TPU v7x, 32 devices: a whole 2x2x4 slice. The times are simulated.
32 devices in a mesh: slab: 8 (over y, x, core), field: 4 (over z).
Axes of the slice: x: 2, y: 2, z: 4, core: 2. Of those that a mesh axis runs over, the one named last changes fastest.
Arguments:
- snaps: bfloat16 [4, 16, 3, 32, 2048], P('field', 'slab'), may hold values from -6 to 6
- writer_map: int32 [64], replicated, may hold values from 0 to 63, each once
- omega: int32 [64, 64], replicated, may hold values from -3 to 3
- face_level: int32 [32], replicated, may hold values from 0 to 11
Outputs:
- sketch_rows: float32 [4, 16, 64], P('field')
- core: float32 [64, 64], replicated
All inputs are finite; a program needn't handle non-finite values.
Results may differ from a plain program's by a relative error of at most 0.00035.
Values may be sent and summed in bfloat16 or wider, within the bound.
A program may use at most 128 MiB of HBM per device.

v0:
```python
import jax
import jax.numpy as jnp
from jax import lax
from jax.sharding import PartitionSpec as P


def from_behind(block, axis, distance):
    devices = range(lax.axis_size(axis))
    route = [(i - distance, i) for i in devices if i - distance in devices]
    return lax.ppermute(block, axis, route)


def body(snaps, writer_map, omega, face_level):
    field_count = lax.axis_size("field")
    slab_at = lax.axis_index("slab")
    field_at = lax.axis_index("field")
    sketch_cols = omega.shape[1]
    total_snaps = omega.shape[0]
    total_planes = face_level.shape[0]
    group_rows = total_snaps // field_count
    columns = jnp.arange(total_snaps, dtype=jnp.int32)
    onehot = (writer_map[:, None] == columns[None, :]).astype(jnp.bfloat16)
    test_all = jnp.dot(
        onehot, omega.astype(jnp.bfloat16), preferred_element_type=jnp.float32
    ).astype(jnp.bfloat16)
    local = lax.all_to_all(snaps, "slab", split_axis=3, concat_axis=1, tiled=True)
    comps = local.shape[2]
    planes_dev = local.shape[3]
    cells = local.shape[4]
    features = comps * planes_dev * cells
    test_own = lax.dynamic_slice_in_dim(test_all, field_at * group_rows, group_rows, 0)
    flat = local.reshape(group_rows, features)
    partial_z = jnp.dot(test_own.T, flat, preferred_element_type=jnp.float32)
    sketched = lax.psum(partial_z.astype(jnp.bfloat16), "field").astype(jnp.float32)
    sketched = sketched.reshape(sketch_cols, comps, planes_dev, cells)
    spacing = 0.5 * jnp.power(jnp.float32(1.12), face_level.astype(jnp.float32))
    first_plane = slab_at * planes_dev
    weight = lax.dynamic_slice_in_dim(spacing, first_plane, planes_dev, 0).reshape(
        1, 1, planes_dev, 1
    )
    coupling = lax.dynamic_slice_in_dim(1.0 / spacing, first_plane, planes_dev, 0).reshape(
        1, 1, planes_dev, 1
    )
    scale = 1.0 / (comps * total_planes * cells)
    lower = from_behind(
        sketched[:, :, -1:].astype(jnp.bfloat16), ("slab", "field"), field_count
    ).astype(jnp.float32)
    below = jnp.concatenate([lower, sketched[:, :, :-1]], axis=2)
    flux = coupling * (sketched - below)
    upper = from_behind(
        flux[:, :, :1].astype(jnp.bfloat16), ("slab", "field"), -field_count
    ).astype(jnp.float32)
    above = jnp.concatenate([flux[:, :, 1:], upper], axis=2)
    applied = (
        ((weight * sketched + flux - above) * scale)
        .astype(jnp.bfloat16)
        .reshape(sketch_cols, features)
    )
    partial_rows = lax.dot_general(
        flat, applied, (((1,), (1,)), ((), ())), preferred_element_type=jnp.float32
    )
    blocks = (jnp.arange(field_count, dtype=jnp.int32) == field_at).astype(jnp.float32)
    stored_rows = (blocks[:, None, None] * partial_rows[None, :, :]).reshape(
        total_snaps, sketch_cols
    )
    rows = lax.psum(stored_rows, ("slab", "field"))
    core = (
        jnp.dot(test_all.astype(jnp.float32).T, rows, precision=lax.Precision.HIGHEST) / total_snaps
    )
    own_rows = lax.dynamic_slice_in_dim(rows, field_at * group_rows, group_rows, 0)
    return (own_rows.reshape(1, group_rows, sketch_cols), core)


def solution(mesh):
    in_specs = (P("field", "slab", None, None, None), P(), P(), P())
    out_specs = (P("field", None, None), P())
    return jax.shard_map(body, mesh=mesh, in_specs=in_specs, out_specs=out_specs, check_vma=False)
```

profile of v0, /device:TPU:0, one launch (start us, length us, event | category | flops | bytes accessed | tf_op | source)
XLA Modules:
  0.0 285.8 jit_solution(11686878091657337957)
XLA Ops:
  7.2 2.8 copy.7
  10.0 5.2 %all-to-all-start = ((bf16[1,2,3,32,2048]{4,2,1,0,3:T(4,128)(2,1)}), bf16[1,2,3,32,2048]{4,2,1,0,3:T(4,128)(2,1)S(1)}, u32[]{:S(2)}, u32[]{:S(2)}) async-start(bf16[1,2,3,32,2048]{4,2,1,0,3:T(4,128)(2,1)} %copy.7), calls=%async_computation | async-start | bytes 2097152 | tf_op jit(solution)/shard_map/all_to_all | solution.py:26
  15.2 1.0 convolution_convert_fusion.1
  16.2 14.4 %all-to-all-done = bf16[1,2,3,32,2048]{4,2,1,0,3:T(4,128)(2,1)S(1)} async-done(((bf16[1,2,3,32,2048]{4,2,1,0,3:T(4,128)(2,1)}), bf16[1,2,3,32,2048]{4,2,1,0,3:T(4,128)(2,1)S(1)}, u32[]{:S(2)}, u32[]{:S(2)}) %all-to-all-start) | async-done | bytes 786464 | tf_op jit(solution)/shard_map/all_to_all | solution.py:26
  30.5 0.9 copy.18
  31.5 0.6 reshape.33
  32.1 2.7 convolution_convert_fusion
  34.8 120.6 %all-reduce.2.cloned.1.call-done = bf16[64,24576]{1,0:T(8,128)(2,1)} async-done(((bf16[64,24576]{1,0:T(8,128)(2,1)}), bf16[64,24576]{1,0:T(8,128)(2,1)}) %all-reduce.2.cloned.1.call-update) | async-done | bytes 3145744 | tf_op jit(solution)/shard_map/psum | solution.py:34
  155.4 7.9 %reshape.34 = f32[64,3,4,2048]{3,2,1,0:T(4,128)} reshape(bf16[64,24576]{1,0:T(8,128)(2,1)} %all-reduce.2.cloned.1.call-done) | data formatting | bytes 9437184 | tf_op jit(solution)/shard_map/reshape | solution.py:35
  163.3 4.5 %slice.25 = bf16[64,3,1,2048]{3,2,1,0:T(2,128)(2,1)S(1)} slice(f32[64,3,4,2048]{3,2,1,0:T(4,128)} %reshape.34), slice={[0:64], [0:3], [3:4], [0:2048]} | slice | bytes 1572864 | tf_op jit(solution)/shard_map/slice | solution.py:46
  167.8 0.5 copy.20
  168.2 1.9 collective-permute-start
  170.3 2.3 slice-done.2
  172.6 2.7 copy.19
  175.4 0.2 convert_element_type.42
  175.6 5.9 %pad_maximum_fusion = (f32[64,3,4,2048]{3,0,2,1:T(8,128)}, f32[64,3,4,2048]{3,0,2,1:T(8,128)S(1)}) fusion(f32[64,3,3,2048]{3,0,2,1:T(8,128)S(1)} %copy.19, f32[64,3,1,2048]{3,0,2,1:T(8,128)S(1)} %convert_element_type.42, f32[64,3,4,2048]{3,2,1,0:T(4,128)S(1)} %bitcast.21, f32[4]{0:T(128)S(1)} %dynamic_slice.14), kind=kLoop, calls=%fused_computation.1 | loop fusion | flops 4718592 | bytes 25165840 | tf_op jit(solution)/shard_map/concatenate | solution.py:48
  181.5 2.8 copy-done
  184.3 0.1 slice.24
  184.4 1.3 collective-permute-start.1
  185.9 0.1 broadcast_bitcast_fusion.1
  186.1 0.1 mul.71
  186.2 5.1 %slice.20 = f32[64,3,3,2048]{3,0,2,1:T(8,128)} slice(f32[64,3,4,2048]{3,0,2,1:T(8,128)} %copy-done), slice={[0:64], [0:3], [1:4], [0:2048]} | slice | bytes 9437184 | tf_op jit(solution)/shard_map/slice | solution.py:53
  191.3 6.7 %copy.11 = f32[64,3,4,2048]{3,2,1,0:T(4,128)} copy(f32[64,3,4,2048]{3,0,2,1:T(8,128)S(1)} %bitcast.23) | data formatting | bytes 12582912 | tf_op jit(solution)/shard_map/concatenate | solution.py:48
  198.0 8.0 %concatenate.11 = f32[64,24576]{1,0:T(8,128)} reshape(f32[64,3,4,2048]{3,2,1,0:T(4,128)} %copy.11) | data formatting | bytes 12582912 | tf_op jit(solution)/shard_map/concatenate | solution.py:48
  206.0 1.3 convert_element_type.43
  207.3 2.8 pad_maximum_fusion.1
  210.1 6.6 %copy.13 = f32[64,3,4,2048]{3,2,1,0:T(4,128)} copy(f32[64,3,4,2048]{3,0,2,1:T(8,128)S(1)} %pad_maximum_fusion.1) | data formatting | bytes 12582912 | tf_op jit(solution)/shard_map/concatenate | solution.py:53
  216.7 8.1 %concatenate.13 = f32[64,24576]{1,0:T(8,128)} reshape(f32[64,3,4,2048]{3,2,1,0:T(4,128)} %copy.13) | data formatting | bytes 12582912 | tf_op jit(solution)/shard_map/concatenate | solution.py:53
  224.8 6.4 %fusion.2 = f32[16,64]{1,0:T(8,128)S(1)} fusion(bf16[16,24576]{1,0:T(8,128)(2,1)} %copy-done.2, f32[64,24576]{1,0:T(8,128)} %concatenate.13, f32[64,24576]{1,0:T(8,128)} %concatenate.11, f32[24576]{0:T(1024)S(1)} %bitcast.26, f32[24576]{0:T(1024)S(1)} %bitcast.27, bf16[64,24576]{1,0:T(8,128)(2,1)S(1)} %copy-done.1), kind=kOutput, calls=%fused_computation.11 | convolution fusion | flops 62914560 | bytes 16715776 | tf_op jit(solution)/shard_map/dot_general | solution.py:59
  231.3 46.2 %psum.15 = f32[64,64]{1,0:T(8,128)S(1)} all-reduce(f32[64,64]{1,0:T(8,128)S(1)} %bitcast_multiply_fusion), channel_id=1, replica_groups=mesh['slab'=8,'field'=4] {'slab','field'}, use_global_device_ids=true, to_apply=%region_1.0 | all-reduce | flops 4096 | bytes 32768 | tf_op jit(solution)/shard_map/psum | solution.py:66
  277.5 0.8 convolution_multiply_fusion
  278.3 0.6 dynamic-slice_bitcast_fusion
  (31 shorter events, 0.5 us)
Async XLA Ops:
  10.0 20.6 %all-to-all-start = ((bf16[1,2,3,32,2048]{4,2,1,0,3:T(4,128)(2,1)}), bf16[1,2,3,32,2048]{4,2,1,0,3:T(4,128)(2,1)S(1)}, u32[]{:S(2)}, u32[]{:S(2)}) async-start(bf16[1,2,3,32,2048]{4,2,1,0,3:T(4,128)(2,1)} %copy.7), calls=%async_computation | async-start | bytes 2097152 | tf_op jit(solution)/shard_map/all_to_all | solution.py:26
  15.1 140.3 %all-reduce.2.cloned.1.call-start = ((), (), s32[]{:S(2)}) async-start(), calls=%async_computation.1 | async-start | bytes 6291456 | tf_op jit(solution)/shard_map/psum | solution.py:34
  32.1 131.2 %copy-start.2 = (bf16[16,24576]{1,0:T(8,128)(2,1)}, bf16[16,24576]{1,0:T(8,128)(2,1)S(1)}, u32[]{:S(2)}) copy-start(bf16[16,24576]{1,0:T(8,128)(2,1)S(1)} %reshape.33) | copy-start | bytes 2359300
  34.8 135.4 %copy-start.3 = (s32[32]{0:T(128)S(1)}, s32[32]{0:T(128)}, u32[]{:S(2)}) copy-start(s32[32]{0:T(128)} %param.7) | copy-start | bytes 388
  168.2 7.1 %collective-permute-start = (bf16[64,3,1,2048]{3,0,2,1:T(8,128)(2,1)S(1)}, bf16[64,3,1,2048]{3,0,2,1:T(8,128)(2,1)S(1)}, u32[]{:S(2)}, u32[]{:S(2)}) collective-permute-start(bf16[64,3,1,2048]{3,0,2,1:T(8,128)(2,1)S(1)} %copy.20), channel_id=1, source_target_pairs={{0,4},{1,5},{2,6},{3,7},{4,8},{5,9},{6,10},{7,11},{8,12},{9,13},{1... | collective-permute-start | bytes 2359304 | tf_op jit(solution)/shard_map/ppermute | solution.py:10
  170.3 2.3 slice-start.2
  170.3 5.3 %slice-start = ((s8[6291456]{0:T(1024)(128)(4,1)}), s8[4194304]{0:T(1024)(128)(4,1)S(1)}, s32[]{:S(2)}) async-start(s8[6291456]{0:T(1024)(128)(4,1)} %bitcast.20), calls=%async_computation.2 | async-start | bytes 8388608
  172.6 2.9 %slice-start.1 = ((s8[6291456]{0:T(1024)(128)(4,1)}), s8[2097152]{0:T(1024)(128)(4,1)S(1)}, s32[]{:S(2)}) async-start(s8[6291456]{0:T(1024)(128)(4,1)} %bitcast.20), calls=%async_computation.3 | async-start | bytes 4194304
  181.5 2.8 copy-start
  181.5 9.9 %slice-start.3 = ((s8[6291456]{0:T(1024)(128)(4,1)}), s8[2097152]{0:T(1024)(128)(4,1)S(1)}, s32[]{:S(2)}) async-start(s8[6291456]{0:T(1024)(128)(4,1)} %bitcast.22), calls=%async_computation.5 | async-start | bytes 4194304
  184.4 21.6 %collective-permute-start.1 = (bf16[64,3,1,2048]{3,0,2,1:T(8,128)(2,1)S(1)}, bf16[64,3,1,2048]{3,0,2,1:T(8,128)(2,1)}, u32[]{:S(2)}, u32[]{:S(2)}) collective-permute-start(bf16[64,3,1,2048]{3,0,2,1:T(8,128)(2,1)S(1)} %slice.24), channel_id=1, source_target_pairs={{4,0},{5,1},{6,2},{7,3},{8,4},{9,5},{10,6},{11,7},{12,8},{13,9},{1... | collective-permute-start | bytes 2359304 | tf_op jit(solution)/shard_map/ppermute | solution.py:10
  186.2 5.1 %slice-start.4 = ((s8[6291456]{0:T(1024)(128)(4,1)}), s8[4194304]{0:T(1024)(128)(4,1)S(1)}, s32[]{:S(2)}) async-start(s8[6291456]{0:T(1024)(128)(4,1)} %bitcast.22), calls=%async_computation.6 | async-start | bytes 8388608
  216.7 8.1 %copy-start.1 = (bf16[64,24576]{1,0:T(8,128)(2,1)S(1)}, bf16[64,24576]{1,0:T(8,128)(2,1)}, u32[]{:S(2)}) copy-start(bf16[64,24576]{1,0:T(8,128)(2,1)} %all-reduce.2.cloned.1.call-done) | copy-start | bytes 9437188
Sparse Core Ops, SparseCore 0:
  34.9 120.4 all-reduce.1
where the time goes:
time: 286 us
  waiting for transfers between devices  135 us (47%)
  local copies, waits for them, and re-layouts  60.8 us (21%)
  blocking collectives  46.2 us (16%)
  between operations  14.2 us (5%)
  matrix products  10.9 us (4%)
  other arithmetic  10.2 us (4%)
  starting transfers between devices  8.43 us (3%)
    psum x1, waiting for transfers between devices, body(): lax.psum(partial_z.astype(jnp.bfloat16), 'field').astype(jnp.float32)  121 us
    psum x1, blocking collectives, body(): rows = lax.psum(stored_rows, ('slab', 'field'))  46.2 us
    concatenate x2, local copies, waits for them, and re-layouts, body(): above = jnp.concatenate([flux[:, :, 1:], upper], axis=2)  14.7 us
    concatenate x2, local copies, waits for them, and re-layouts, body(): below = jnp.concatenate([lower, sketched[:, :, :-1]], axis=2)  14.6 us
    all_to_all x1, waiting for transfers between devices, body(): lax.all_to_all(snaps, 'slab', split_axis=3, concat_axis=1, tiled=True)  14.4 us
    unnamed x23, local copies, waits for them, and re-layouts  9.04 us
    reshape x1, local copies, waits for them, and re-layouts, body(): sketched = sketched.reshape(sketch_cols, comps, planes_dev, cells)  7.87 us
    dot_general x1, matrix products, body(): lax.dot_general(flat, applied, (((1,), (1,)), ((), ())), preferred_elemen...  6.4 us
  transfers between devices with their start and end apart: 4, of which 2 were waited for; matrix products, arithmetic and copies ran while one was open for 8% of the time, Pallas kernels for 0%

commit v1 on v0

v1 whole, which is shorter than its diff:
```python
import functools

import jax
import jax.numpy as jnp
import numpy as np
from jax import lax
from jax.experimental import pallas as pl
from jax.experimental.pallas import tpu as pltpu
from jax.sharding import PartitionSpec as P

MESH = pl.DeviceIdType.MESH
LANES = 128


def split3(value):
    high = value.astype(jnp.bfloat16)
    rest = value - high.astype(jnp.float32)
    mid = rest.astype(jnp.bfloat16)
    low = (rest - mid.astype(jnp.float32)).astype(jnp.bfloat16)
    return high, mid, low


def kernel(
    slabs,
    fields,
    snaps_ref,
    map_ref,
    omega_ref,
    level_ref,
    rows_ref,
    core_ref,
    x_ref,
    send_ref,
    recv_ref,
    wide_ref,
    xb_ref,
    vb_ref,
    coef_ref,
    part_ref,
    slab_ref,
    field_ref,
    full_ref,
    load_sem,
    send_sem,
    recv_sem,
    small_send,
    small_recv,
):
    devices = slabs * fields
    local, comps, planes, cells = x_ref.shape
    groups = LANES * devices // cells
    width = LANES // groups
    rows = planes // groups
    tiles = cells // LANES
    total = devices * local
    cols = omega_ref.shape[1]
    slab = lax.axis_index("slab")
    field = lax.axis_index("field")
    me = field * slabs + slab

    loads = [
        pltpu.make_async_copy(snaps_ref.at[0, :, a], x_ref.at[:, a], load_sem.at[a])
        for a in range(comps)
    ]
    for load in loads:
        load.start()

    barrier = pltpu.get_barrier_semaphore()

    def greet(k, carry):
        there = (me + k) % devices
        pl.semaphore_signal(
            barrier,
            inc=1,
            device_id={"slab": there % slabs, "field": there // slabs},
            device_id_type=MESH,
        )
        return carry

    lax.fori_loop(1, devices, greet, 0)

    def stage(a):
        for i in range(local):
            for t in range(tiles):
                parts = [
                    x_ref[i, a, g * rows : (g + 1) * rows, t * LANES : (t + 1) * LANES]
                    for g in range(groups)
                ]
                for q in range(groups):
                    send_ref[a, t * groups + q, i] = jnp.concatenate(
                        [p[:, q * width : (q + 1) * width] for p in parts], axis=1
                    )

    def send(a, ks, kf):
        to_slab = (slab + ks) % slabs
        to_field = (field + kf) % fields
        pltpu.make_async_remote_copy(
            src_ref=send_ref.at[a, to_field * slabs + to_slab],
            dst_ref=recv_ref.at[a, me],
            send_sem=send_sem.at[a],
            recv_sem=recv_sem.at[a],
            device_id={"slab": to_slab, "field": to_field},
            device_id_type=MESH,
        ).start()

    order = [k for k in (2, 1, 3, 0) if k < fields]

    def send_all(a):
        for kf in order:
            if kf:
                send(a, 0, kf)

        def step(ks, carry):
            for kf in order:
                send(a, ks, kf)
            return carry

        lax.fori_loop(1, slabs, step, 0)

    for a in range(comps):
        loads[a].wait()
        stage(a)
        recv_ref[a, me] = send_ref[a, me]
        if a == 0:
            pl.semaphore_wait(barrier, devices - 1)
        send_all(a)

    time = lax.broadcasted_iota(jnp.int32, (total, total), 0)
    onehot = (time == map_ref[...]).astype(jnp.float32).astype(jnp.bfloat16)
    omega = omega_ref[...].astype(jnp.float32).astype(jnp.bfloat16)
    test = lax.dot_general(
        onehot, omega, (((0,), (0,)), ((), ())), preferred_element_type=jnp.float32
    ).astype(jnp.bfloat16)
    test_t = lax.dot_general(
        omega, onehot, (((0,), (0,)), ((), ())), preferred_element_type=jnp.float32
    ).astype(jnp.bfloat16)

    scale = 1.0 / (comps * planes * cells)
    spacing = 0.5 * jnp.exp(level_ref[...].astype(jnp.float32) * np.float32(np.log(1.12)))
    inverse = 1.0 / spacing
    row_at = lax.broadcasted_iota(jnp.int32, (rows, planes), 0)
    plane_at = lax.broadcasted_iota(jnp.int32, (rows, planes), 1)
    lane_group = lax.broadcasted_iota(jnp.int32, (rows, LANES), 1) // width

    def pick(values, shift):
        out = jnp.zeros((rows, LANES), jnp.float32)
        for g in range(groups):
            hit = plane_at == row_at + (g * rows + shift)
            column = jnp.sum(jnp.where(hit, values, 0.0), axis=1, keepdims=True)
            out = jnp.where(lane_group == g, column, out)
        return out

    lower = pick(inverse, 0) * scale
    upper = pick(inverse, 1) * scale
    coef_ref[0] = pick(spacing, 0) * scale + lower + upper
    coef_ref[1] = lower
    coef_ref[2] = upper

    lane = lax.broadcasted_iota(jnp.int32, (total, LANES), 1)
    gram = None
    for a in range(comps):
        arrived = recv_ref.at[a, pl.ds(0, devices - 1)]
        pltpu.make_async_copy(arrived, arrived, recv_sem.at[a]).wait()

        def widen(d, carry):
            wide_ref[pl.ds(d * (local * rows), local * rows), :] = (
                recv_ref[a, d].reshape(local * rows, LANES).astype(jnp.float32)
            )
            return carry

        lax.fori_loop(0, devices, widen, 0, unroll=8)

        def load_row(j):
            return wide_ref[pl.ds(j, total, stride=rows), :]

        first = load_row(0)
        last = load_row(rows - 1)
        below = jnp.where(lane < width, 0.0, pltpu.roll(last, width, 1))
        here = first
        for j in range(rows):
            if j + 1 < rows:
                above = load_row(j + 1)
            else:
                above = jnp.where(
                    lane >= LANES - width, 0.0, pltpu.roll(first, LANES - width, 1)
                )
            applied = (
                coef_ref[0, j : j + 1, :] * here
                - coef_ref[1, j : j + 1, :] * below
                - coef_ref[2, j : j + 1, :] * above
            )
            xb_ref[:, j * LANES : (j + 1) * LANES] = here.astype(jnp.bfloat16)
            vb_ref[:, j * LANES : (j + 1) * LANES] = applied.astype(jnp.bfloat16)
            below, here = here, above
        term = lax.dot_general(
            xb_ref[...],
            vb_ref[...],
            (((1,), (1,)), ((), ())),
            preferred_element_type=jnp.float32,
        )
        gram = term if gram is None else gram + term

    pad = jnp.zeros((total, LANES - cols), jnp.float32)
    wide_test = jnp.concatenate([test.astype(jnp.float32), pad], axis=1).astype(jnp.bfloat16)
    partial = sum(
        jnp.dot(piece, wide_test, preferred_element_type=jnp.float32) for piece in split3(gram)
    )
    block = total // slabs
    part_ref[...] = partial.reshape(slabs, block, LANES)

    def small(src, dst, phase, to_slab, to_field):
        pltpu.make_async_remote_copy(
            src_ref=src,
            dst_ref=dst,
            send_sem=small_send.at[phase],
            recv_sem=small_recv.at[phase],
            device_id={"slab": to_slab, "field": to_field},
            device_id_type=MESH,
        ).start()

    def await_all(ref, count, phase):
        some = ref.at[pl.ds(0, count)]
        pltpu.make_async_copy(some, some, small_recv.at[phase]).wait()

    for ks in range(1, slabs):
        to = (slab + ks) % slabs
        small(part_ref.at[to], slab_ref.at[slab], 0, to, field)
    slab_ref[slab] = part_ref[slab]
    await_all(slab_ref, slabs - 1, 0)
    field_ref[field] = jnp.sum(slab_ref[...], axis=0)
    for kf in range(1, fields):
        small(field_ref.at[field], field_ref.at[field], 1, slab, (field + kf) % fields)
    await_all(field_ref, fields - 1, 1)
    full_ref[slab] = jnp.sum(field_ref[...], axis=0)
    for ks in range(1, slabs):
        small(full_ref.at[slab], full_ref.at[slab], 2, (slab + ks) % slabs, field)
    await_all(full_ref, slabs - 1, 2)

    blocks = slabs // fields
    own = full_ref[pl.ds(field * blocks, blocks)].reshape(total // fields, LANES)
    rows_ref[0] = own[:, :cols]
    sketch = full_ref[...].reshape(total, LANES)[:, :cols]
    core_ref[...] = (
        sum(jnp.dot(test_t, piece, preferred_element_type=jnp.float32) for piece in split3(sketch))
        / total
    )

    for a in range(comps):
        sent = send_ref.at[a, pl.ds(0, devices - 1)]
        pltpu.make_async_copy(sent, sent, send_sem.at[a]).wait()
    for phase, count in ((0, slabs - 1), (2, slabs - 1)):
        sent = slab_ref.at[pl.ds(0, count)]
        pltpu.make_async_copy(sent, sent, small_send.at[phase]).wait()
    sent = field_ref.at[pl.ds(0, fields - 1)]
    pltpu.make_async_copy(sent, sent, small_send.at[1]).wait()


def body(snaps, writer_map, omega, face_level):
    slabs = lax.axis_size("slab")
    fields = lax.axis_size("field")
    devices = slabs * fields
    _, local, comps, planes, cells = snaps.shape
    total, cols = omega.shape
    groups = LANES * devices // cells
    rows = planes // groups
    block = total // slabs
    chunk = (comps, devices, local, rows, LANES)
    vmem = pl.BlockSpec(memory_space=pltpu.VMEM)
    return pl.pallas_call(
        functools.partial(kernel, slabs, fields),
        out_shape=(
            jax.ShapeDtypeStruct((1, total // fields, cols), jnp.float32),
            jax.ShapeDtypeStruct((cols, cols), jnp.float32),
        ),
        in_specs=[pl.BlockSpec(memory_space=pl.ANY), vmem, vmem, vmem],
        out_specs=(vmem, vmem),
        scratch_shapes=[
            pltpu.VMEM((local, comps, planes, cells), jnp.bfloat16),
            pltpu.VMEM(chunk, jnp.bfloat16),
            pltpu.VMEM(chunk, jnp.bfloat16),
            pltpu.VMEM((total * rows, LANES), jnp.float32),
            pltpu.VMEM((total, rows * LANES), jnp.bfloat16),
            pltpu.VMEM((total, rows * LANES), jnp.bfloat16),
            pltpu.VMEM((3, rows, LANES), jnp.float32),
            pltpu.VMEM((slabs, block, LANES), jnp.float32),
            pltpu.VMEM((slabs, block, LANES), jnp.float32),
            pltpu.VMEM((fields, block, LANES), jnp.float32),
            pltpu.VMEM((slabs, block, LANES), jnp.float32),
            pltpu.SemaphoreType.DMA((comps,)),
            pltpu.SemaphoreType.DMA((comps,)),
            pltpu.SemaphoreType.DMA((comps,)),
            pltpu.SemaphoreType.DMA((3,)),
            pltpu.SemaphoreType.DMA((3,)),
        ],
        compiler_params=pltpu.CompilerParams(
            collective_id=0, has_side_effects=True, vmem_limit_bytes=40 * 1024 * 1024
        ),
    )(snaps, writer_map.reshape(1, total), omega, face_level.reshape(1, planes))


def solution(mesh):
    in_specs = (P("field", "slab", None, None, None), P(), P(), P())
    out_specs = (P("field", None, None), P())
    return jax.shard_map(body, mesh=mesh, in_specs=in_specs, out_specs=out_specs, check_vma=False)
```

time: 286 us -> 41.2 us (0.14)
  waiting for transfers between devices: 135 us -> 0 us
  local copies, waits for them, and re-layouts: 60.8 us -> 3.76 us
  blocking collectives: 46.2 us -> 0 us
  Pallas kernels: 0 us -> 36.6 us
  between operations: 14.2 us -> 0.66 us
  matrix products: 10.9 us -> 0 us
  other arithmetic: 10.2 us -> 0 us
  starting transfers between devices: 8.43 us -> 0 us
    psum x1 -> x0, waiting for transfers between devices: 121 us -> none  [body(): lax.psum(partial_z.astype(jnp.bfloat16), 'field').astype(jnp.float32)]
    psum x1 -> x0, blocking collectives: 46.2 us -> none  [body(): rows = lax.psum(stored_rows, ('slab', 'field'))]
    pallas_call x0 -> x1, Pallas kernels: none -> 36.6 us  [body(): pl.pallas_call(functools.partial(kernel, slabs, fields), out_shape=(jax.S...]
    concatenate x4 -> x0, local copies, waits for them, and re-layouts: 29.4 us -> none  [the longest x2 14.7 us: body(): above = jnp.concatenate([flux[:, :, 1:], upper], axis=2)]
    all_to_all x1 -> x0, waiting for transfers between devices: 14.4 us -> none  [body(): lax.all_to_all(snaps, 'slab', split_axis=3, concat_axis=1, tiled=True)]
    slice x5 -> x0, local copies, waits for them, and re-layouts: 12.1 us -> none  [the longest x1 5.14 us: body(): above = jnp.concatenate([flux[:, :, 1:], upper], axis=2)]
    dot_general x4 -> x0, matrix products: 10.9 us -> none  [the longest x1 6.4 us: body(): lax.dot_general(flat, applied, (((1,), (1,)), ((), ())), preferred_elemen...]
    reshape x3 -> x0, local copies, waits for them, and re-layouts: 9.05 us -> none  [the longest x1 7.87 us: body(): sketched = sketched.reshape(sketch_cols, comps, planes_dev, cells)]
  transfers between devices with their start and end apart: 4 -> 0, of which waited for: 2 -> 0; matrix products, arithmetic and copies ran while one was open for 8% -> 0% of each run, Pallas kernels for 0% -> 0%
where the time goes in v1:
time: 41.2 us; the launch traced here: 41 us
  Pallas kernels  36.6 us (89%)
  local copies, waits for them, and re-layouts  3.76 us (9%)
  between operations  0.66 us (2%)
    pallas_call x1, Pallas kernels, body(): pl.pallas_call(functools.partial(kernel, slabs, fields), out_shape=(jax.S...  36.6 us
    unnamed x10, local copies, waits for them, and re-layouts  3.76 us

profile of v1, /device:TPU:0, one launch (start us, length us, event | category | flops | bytes accessed | tf_op | source)
XLA Modules:
  0.0 41.0 jit_solution(8789890009606477396)
XLA Ops:
  0.6 0.0 copy-start.2
  0.6 0.0 copy-start.3
  0.7 0.6 %copy-done.2 = s32[64]{0:T(128)S(1)} copy-done((s32[64]{0:T(128)S(1)}, s32[64]{0:T(128)}, u32[]{:S(2)}) %copy-start.2) | copy-done | bytes 280
  1.3 0.0 copy-done.3
  1.3 0.0 copy-start
  1.3 1.1 %copy-done = bf16[1,2,3,32,2048]{4,3,2,1,0:T(8,128)(2,1)S(1)} copy-done((bf16[1,2,3,32,2048]{4,3,2,1,0:T(8,128)(2,1)S(1)}, bf16[1,2,3,32,2048]{4,3,2,1,0:T(8,128)(2,1)}, u32[]{:S(2)}) %copy-start) | copy-done | bytes 786456
  2.4 0.0 copy-start.1
  2.4 0.8 %copy-done.1 = s32[64,64]{1,0:T(8,128)S(1)} copy-done((s32[64,64]{1,0:T(8,128)S(1)}, s32[64,64]{1,0:T(8,128)}, u32[]{:S(2)}) %copy-start.1) | copy-done | bytes 16408
  3.2 36.6 %shard_map.59 = (f32[1,16,64]{2,1,0:T(8,128)S(1)}, f32[64,64]{1,0:T(8,128)S(1)}) custom-call(bf16[1,2,3,32,2048]{4,3,2,1,0:T(8,128)(2,1)S(1)} %copy-done, s32[1,64]{1,0:T(1,128)S(1)} %bitcast.2, s32[64,64]{1,0:T(8,128)S(1)} %copy-done.1, s32[1,32]{1,0:T(1,128)S(1)} %bitcast.3), custom_call_target="tpu_custom_call" | custom-call | tf_op jit(solution)/shard_map/pallas_call | solution.py:269
  39.8 0.6 %copy.8 = f32[1,16,64]{2,1,0:T(8,128)} copy(f32[1,16,64]{2,1,0:T(8,128)S(1)} %get-tuple-element.4) | data formatting | bytes 8192
  40.4 0.6 %copy.9 = f32[64,64]{1,0:T(8,128)} copy(f32[64,64]{1,0:T(8,128)S(1)} %get-tuple-element.5) | data formatting | bytes 32768
Async XLA Ops:
  0.6 0.7 %copy-start.2 = (s32[64]{0:T(128)S(1)}, s32[64]{0:T(128)}, u32[]{:S(2)}) copy-start(s32[64]{0:T(128)} %param.5) | copy-start | bytes 772
  0.6 0.7 %copy-start.3 = (s32[32]{0:T(128)S(1)}, s32[32]{0:T(128)}, u32[]{:S(2)}) copy-start(s32[32]{0:T(128)} %param.7) | copy-start | bytes 388
  1.3 1.1 %copy-start = (bf16[1,2,3,32,2048]{4,3,2,1,0:T(8,128)(2,1)S(1)}, bf16[1,2,3,32,2048]{4,3,2,1,0:T(8,128)(2,1)}, u32[]{:S(2)}) copy-start(bf16[1,2,3,32,2048]{4,3,2,1,0:T(8,128)(2,1)} %snaps_ref.1) | copy-start | bytes 2359300
  2.4 0.8 %copy-start.1 = (s32[64,64]{1,0:T(8,128)S(1)}, s32[64,64]{1,0:T(8,128)}, u32[]{:S(2)}) copy-start(s32[64,64]{1,0:T(8,128)} %omega_ref.1) | copy-start | bytes 49156

commit v2 on v1

--- a/solution.py
+++ b/solution.py
@@ -24,12 +24,15 @@
     slabs,
     fields,
     snaps_ref,
+    map_hbm,
+    omega_hbm,
+    level_hbm,
+    rows_ref,
+    core_ref,
+    x_ref,
     map_ref,
     omega_ref,
     level_ref,
-    rows_ref,
-    core_ref,
-    x_ref,
     send_ref,
     recv_ref,
     wide_ref,
@@ -37,10 +40,10 @@
     vb_ref,
     coef_ref,
     part_ref,
-    slab_ref,
-    field_ref,
+    sum_ref,
     full_ref,
     load_sem,
+    table_sem,
     send_sem,
     recv_sem,
     small_send,
@@ -62,7 +65,13 @@
         pltpu.make_async_copy(snaps_ref.at[0, :, a], x_ref.at[:, a], load_sem.at[a])
         for a in range(comps)
     ]
-    for load in loads:
+    tables = [
+        pltpu.make_async_copy(src, dst, table_sem.at[n])
+        for n, (src, dst) in enumerate(
+            ((map_hbm, map_ref), (omega_hbm, omega_ref), (level_hbm, level_ref))
+        )
+    ]
+    for load in loads + tables:
         load.start()
 
     barrier = pltpu.get_barrier_semaphore()
@@ -124,6 +133,9 @@
         if a == 0:
             pl.semaphore_wait(barrier, devices - 1)
         send_all(a)
+
+    for table in tables:
+        table.wait()
 
     time = lax.broadcasted_iota(jnp.int32, (total, total), 0)
     onehot = (time == map_ref[...]).astype(jnp.float32).astype(jnp.bfloat16)
@@ -200,13 +212,18 @@
         )
         gram = term if gram is None else gram + term
 
-    pad = jnp.zeros((total, LANES - cols), jnp.float32)
-    wide_test = jnp.concatenate([test.astype(jnp.float32), pad], axis=1).astype(jnp.bfloat16)
+    twice = jnp.concatenate([test.astype(jnp.float32)] * 2, axis=1).astype(jnp.bfloat16)
     partial = sum(
-        jnp.dot(piece, wide_test, preferred_element_type=jnp.float32) for piece in split3(gram)
+        jnp.dot(piece, twice, preferred_element_type=jnp.float32) for piece in split3(gram)
     )
-    block = total // slabs
-    part_ref[...] = partial.reshape(slabs, block, LANES)
+    adders = slabs // 2
+    half = total // slabs
+    left = lax.broadcasted_iota(jnp.int32, (half, LANES), 1) < cols
+    for b in range(adders):
+        top = 2 * b * half
+        part_ref[b] = jnp.where(
+            left, partial[top : top + half], partial[top + half : top + 2 * half]
+        )
 
     def small(src, dst, phase, to_slab, to_field):
         pltpu.make_async_remote_copy(
@@ -218,41 +235,61 @@
             device_id_type=MESH,
         ).start()
 
-    def await_all(ref, count, phase):
+    def wait_blocks(ref, count, sem):
         some = ref.at[pl.ds(0, count)]
-        pltpu.make_async_copy(some, some, small_recv.at[phase]).wait()
-
-    for ks in range(1, slabs):
-        to = (slab + ks) % slabs
-        small(part_ref.at[to], slab_ref.at[slab], 0, to, field)
-    slab_ref[slab] = part_ref[slab]
-    await_all(slab_ref, slabs - 1, 0)
-    field_ref[field] = jnp.sum(slab_ref[...], axis=0)
-    for kf in range(1, fields):
-        small(field_ref.at[field], field_ref.at[field], 1, slab, (field + kf) % fields)
-    await_all(field_ref, fields - 1, 1)
-    full_ref[slab] = jnp.sum(field_ref[...], axis=0)
-    for ks in range(1, slabs):
-        small(full_ref.at[slab], full_ref.at[slab], 2, (slab + ks) % slabs, field)
-    await_all(full_ref, slabs - 1, 2)
-
-    blocks = slabs // fields
-    own = full_ref[pl.ds(field * blocks, blocks)].reshape(total // fields, LANES)
-    rows_ref[0] = own[:, :cols]
-    sketch = full_ref[...].reshape(total, LANES)[:, :cols]
+        pltpu.make_async_copy(some, some, sem).wait()
+
+    mine = slab // 2
+    adds = slab % 2 == 0
+    for kf in order:
+        for kb in range(adders):
+            b = (mine + kb) % adders
+            to_field = (field + kf) % fields
+            if kf or kb:
+                small(part_ref.at[b], sum_ref.at[me], 0, 2 * b, to_field)
+
+    @pl.when(slab % 2 == 1)
+    def _():
+        small(part_ref.at[mine], sum_ref.at[me], 0, slab - 1, field)
+
+    @pl.when(adds)
+    def _():
+        sum_ref[me] = part_ref[mine]
+        wait_blocks(sum_ref, devices - 1, small_recv.at[0])
+        full_ref[mine] = jnp.sum(sum_ref[...], axis=0)
+        for ks in range(1, slabs):
+            small(full_ref.at[mine], full_ref.at[mine], 1, (slab + ks) % slabs, field)
+        wait_blocks(full_ref, adders - 1, small_recv.at[1])
+
+    @pl.when(slab % 2 == 1)
+    def _():
+        wait_blocks(full_ref, adders, small_recv.at[1])
+
+    def unpack(blocks, count):
+        pieces = []
+        for b in range(count):
+            pieces += [blocks[b][:, :cols], blocks[b][:, cols : 2 * cols]]
+        return jnp.concatenate(pieces, axis=0)
+
+    held = adders // fields
+    rows_ref[0] = unpack(full_ref[pl.ds(field * held, held)], held)
+    sketch = unpack(full_ref[...], adders)
     core_ref[...] = (
         sum(jnp.dot(test_t, piece, preferred_element_type=jnp.float32) for piece in split3(sketch))
         / total
     )
 
     for a in range(comps):
-        sent = send_ref.at[a, pl.ds(0, devices - 1)]
-        pltpu.make_async_copy(sent, sent, send_sem.at[a]).wait()
-    for phase, count in ((0, slabs - 1), (2, slabs - 1)):
-        sent = slab_ref.at[pl.ds(0, count)]
-        pltpu.make_async_copy(sent, sent, small_send.at[phase]).wait()
-    sent = field_ref.at[pl.ds(0, fields - 1)]
-    pltpu.make_async_copy(sent, sent, small_send.at[1]).wait()
+        wait_blocks(send_ref.at[a], devices - 1, send_sem.at[a])
+    wait_blocks(sum_ref, adders * fields - 1, small_send.at[0])
+
+    @pl.when(slab % 2 == 1)
+    def _():
+        wait_blocks(sum_ref, 1, small_send.at[0])
+
+    @pl.when(adds)
+    def _():
+        wait_blocks(sum_ref, slabs - 1, small_send.at[1])
 
 
 def body(snaps, writer_map, omega, face_level):
@@ -263,7 +300,7 @@
     total, cols = omega.shape
     groups = LANES * devices // cells
     rows = planes // groups
-    block = total // slabs
+    half = total // slabs
     chunk = (comps, devices, local, rows, LANES)
     vmem = pl.BlockSpec(memory_space=pltpu.VMEM)
     return pl.pallas_call(
@@ -272,28 +309,31 @@
             jax.ShapeDtypeStruct((1, total // fields, cols), jnp.float32),
             jax.ShapeDtypeStruct((cols, cols), jnp.float32),
         ),
-        in_specs=[pl.BlockSpec(memory_space=pl.ANY), vmem, vmem, vmem],
+        in_specs=[pl.BlockSpec(memory_space=pltpu.HBM)] * 4,
         out_specs=(vmem, vmem),
         scratch_shapes=[
             pltpu.VMEM((local, comps, planes, cells), jnp.bfloat16),
+            pltpu.VMEM((1, total), jnp.int32),
+            pltpu.VMEM((total, cols), jnp.int32),
+            pltpu.VMEM((1, planes), jnp.int32),
             pltpu.VMEM(chunk, jnp.bfloat16),
             pltpu.VMEM(chunk, jnp.bfloat16),
             pltpu.VMEM((total * rows, LANES), jnp.float32),
             pltpu.VMEM((total, rows * LANES), jnp.bfloat16),
             pltpu.VMEM((total, rows * LANES), jnp.bfloat16),
             pltpu.VMEM((3, rows, LANES), jnp.float32),
-            pltpu.VMEM((slabs, block, LANES), jnp.float32),
-            pltpu.VMEM((slabs, block, LANES), jnp.float32),
-            pltpu.VMEM((fields, block, LANES), jnp.float32),
-            pltpu.VMEM((slabs, block, LANES), jnp.float32),
+            pltpu.VMEM((slabs // 2, half, LANES), jnp.float32),
+            pltpu.VMEM((devices, half, LANES), jnp.float32),
+            pltpu.VMEM((slabs // 2, half, LANES), jnp.float32),
+            pltpu.SemaphoreType.DMA((comps,)),
+            pltpu.SemaphoreType.DMA((3,)),
             pltpu.SemaphoreType.DMA((comps,)),
             pltpu.SemaphoreType.DMA((comps,)),
-            pltpu.SemaphoreType.DMA((comps,)),
-            pltpu.SemaphoreType.DMA((3,)),
-            pltpu.SemaphoreType.DMA((3,)),
+            pltpu.SemaphoreType.DMA((2,)),
+            pltpu.SemaphoreType.DMA((2,)),
         ],
         compiler_params=pltpu.CompilerParams(
-            collective_id=0, has_side_effects=True, vmem_limit_bytes=40 * 1024 * 1024
+            collective_id=0, has_side_effects=True, vmem_limit_bytes=60 * 1024 * 1024
         ),
     )(snaps, writer_map.reshape(1, total), omega, face_level.reshape(1, planes))
 

time: 41.2 us -> 38.9 us (0.944)
  Pallas kernels: 36.6 us -> 35.3 us
  local copies, waits for them, and re-layouts: 3.76 us -> 2.67 us
    pallas_call x1, Pallas kernels: 36.6 us -> 35.3 us  [body(): pl.pallas_call(functools.partial(kernel, slabs, fields), out_shape=(jax.S...]
    unnamed x10 -> x2, local copies, waits for them, and re-layouts: 3.76 us -> 2.67 us
where the time goes in v2:
time: 38.9 us; the launch traced here: 38.6 us
  Pallas kernels  35.3 us (91%)
  local copies, waits for them, and re-layouts  2.67 us (7%)
  between operations  0.64 us (2%)
    pallas_call x1, Pallas kernels, body(): pl.pallas_call(functools.partial(kernel, slabs, fields), out_shape=(jax.S...  35.3 us
    unnamed x2, local copies, waits for them, and re-layouts  2.67 us

profile of v2, /device:TPU:0, one launch (start us, length us, event | category | flops | bytes accessed | tf_op | source)
XLA Modules:
  0.0 38.6 jit_solution(1082181170893367703)
XLA Ops:
  0.6 35.3 %shard_map.59 = (f32[1,16,64]{2,1,0:T(8,128)}, f32[64,64]{1,0:T(8,128)}) custom-call(bf16[1,2,3,32,2048]{4,3,2,1,0:T(8,128)(2,1)} %snaps_ref.1, s32[1,64]{1,0:T(1,128)} %bitcast.2, s32[64,64]{1,0:T(8,128)} %omega_hbm.1, s32[1,32]{1,0:T(1,128)} %bitcast.3), custom_call_target="tpu_custom_call" | custom-call | tf_op jit(solution)/shard_map/pallas_call | solution.py:306
  36.0 1.3 %copy.8 = f32[1,16,64]{2,1,0:T(8,128)} copy(f32[1,16,64]{2,1,0:T(8,128)} %get-tuple-element.4) | data formatting | bytes 8192
  37.3 1.4 %copy.9 = f32[64,64]{1,0:T(8,128)} copy(f32[64,64]{1,0:T(8,128)} %get-tuple-element.5) | data formatting | bytes 32768

commit v3 on v2

--- a/solution.py
+++ b/solution.py
@@ -292,6 +292,17 @@
         wait_blocks(sum_ref, slabs - 1, small_send.at[1])
 
 
+def hand_on(rows_in, core_in, rows_out, core_out, sems):
+    copies = [
+        pltpu.make_async_copy(rows_in, rows_out, sems.at[0]),
+        pltpu.make_async_copy(core_in, core_out, sems.at[1]),
+    ]
+    for copy in copies:
+        copy.start()
+    for copy in copies:
+        copy.wait()
+
+
 def body(snaps, writer_map, omega, face_level):
     slabs = lax.axis_size("slab")
     fields = lax.axis_size("field")
@@ -303,13 +314,15 @@
     half = total // slabs
     chunk = (comps, devices, local, rows, LANES)
     vmem = pl.BlockSpec(memory_space=pltpu.VMEM)
-    return pl.pallas_call(
+    hbm = pl.BlockSpec(memory_space=pltpu.HBM)
+    out_shape = (
+        jax.ShapeDtypeStruct((1, total // fields, cols), jnp.float32),
+        jax.ShapeDtypeStruct((cols, cols), jnp.float32),
+    )
+    results = pl.pallas_call(
         functools.partial(kernel, slabs, fields),
-        out_shape=(
-            jax.ShapeDtypeStruct((1, total // fields, cols), jnp.float32),
-            jax.ShapeDtypeStruct((cols, cols), jnp.float32),
-        ),
-        in_specs=[pl.BlockSpec(memory_space=pltpu.HBM)] * 4,
+        out_shape=out_shape,
+        in_specs=[hbm] * 4,
         out_specs=(vmem, vmem),
         scratch_shapes=[
             pltpu.VMEM((local, comps, planes, cells), jnp.bfloat16),
@@ -336,6 +349,14 @@
             collective_id=0, has_side_effects=True, vmem_limit_bytes=60 * 1024 * 1024
         ),
     )(snaps, writer_map.reshape(1, total), omega, face_level.reshape(1, planes))
+    return pl.pallas_call(
+        hand_on,
+        out_shape=out_shape,
+        in_specs=[hbm] * 2,
+        out_specs=(hbm, hbm),
+        scratch_shapes=[pltpu.SemaphoreType.DMA((2,))],
+        compiler_params=pltpu.CompilerParams(vmem_limit_bytes=60 * 1024 * 1024),
+    )(*results)
 
 
 def solution(mesh):

time: 38.9 us -> 38.5 us (0.990)
  local copies, waits for them, and re-layouts: 2.67 us -> 0 us
  Pallas kernels: 35.3 us -> 37.7 us
    unnamed x2 -> x0, local copies, waits for them, and re-layouts: 2.67 us -> none
    pallas_call x1 -> x2, Pallas kernels: 35.3 us -> 37.7 us  [the longest x1 35.3 us: body(): pl.pallas_call(functools.partial(kernel, slabs, fields), out_shape=out_sh...]
where the time goes in v3:
time: 38.5 us; the launch traced here: 38.3 us
  Pallas kernels  37.7 us (98%)
  between operations  0.64 us (2%)
    pallas_call x1, Pallas kernels, body(): pl.pallas_call(functools.partial(kernel, slabs, fields), out_shape=out_sh...  35.3 us
    pallas_call x1, Pallas kernels, body(): pl.pallas_call(hand_on, out_shape=out_shape, in_specs=[hbm] * 2, out_spec...  2.36 us

profile of v3, /device:TPU:0, one launch (start us, length us, event | category | flops | bytes accessed | tf_op | source)
XLA Modules:
  0.0 38.3 jit_solution(10699012317827620593)
XLA Ops:
  0.6 35.3 %shard_map.59 = (f32[1,16,64]{2,1,0:T(8,128)}, f32[64,64]{1,0:T(8,128)}) custom-call(bf16[1,2,3,32,2048]{4,3,2,1,0:T(8,128)(2,1)} %snaps_ref.1, s32[1,64]{1,0:T(1,128)} %bitcast.2, s32[64,64]{1,0:T(8,128)} %omega_hbm.1, s32[1,32]{1,0:T(1,128)} %bitcast.3), custom_call_target="tpu_custom_call" | custom-call | tf_op jit(solution)/shard_map/pallas_call | solution.py:322
  36.0 2.4 %shard_map.60 = (f32[1,16,64]{2,1,0:T(8,128)}, f32[64,64]{1,0:T(8,128)}) custom-call(f32[1,16,64]{2,1,0:T(8,128)} %get-tuple-element.4.rows_in, f32[64,64]{1,0:T(8,128)} %get-tuple-element.5.core_in), custom_call_target="tpu_custom_call" | custom-call | tf_op jit(solution)/shard_map/pallas_call | solution.py:352

commit v4 on v3

--- a/solution.py
+++ b/solution.py
@@ -292,15 +292,17 @@
         wait_blocks(sum_ref, slabs - 1, small_send.at[1])
 
 
-def hand_on(rows_in, core_in, rows_out, core_out, sems):
-    copies = [
-        pltpu.make_async_copy(rows_in, rows_out, sems.at[0]),
-        pltpu.make_async_copy(core_in, core_out, sems.at[1]),
-    ]
-    for copy in copies:
-        copy.start()
-    for copy in copies:
-        copy.wait()
+def hand_on(rows_in, core_in, rows_out, core_out, rows_held, core_held, in_sems, out_sems):
+    steps = ((rows_in, rows_held, rows_out), (core_in, core_held, core_out))
+    loads = [pltpu.make_async_copy(a, b, in_sems.at[n]) for n, (a, b, c) in enumerate(steps)]
+    stores = [pltpu.make_async_copy(b, c, out_sems.at[n]) for n, (a, b, c) in enumerate(steps)]
+    for load in loads:
+        load.start()
+    for load, store in zip(loads, stores):
+        load.wait()
+        store.start()
+    for store in stores:
+        store.wait()
 
 
 def body(snaps, writer_map, omega, face_level):
@@ -354,7 +356,12 @@
         out_shape=out_shape,
         in_specs=[hbm] * 2,
         out_specs=(hbm, hbm),
-        scratch_shapes=[pltpu.SemaphoreType.DMA((2,))],
+        scratch_shapes=[
+            pltpu.VMEM(out_shape[0].shape, jnp.float32),
+            pltpu.VMEM(out_shape[1].shape, jnp.float32),
+            pltpu.SemaphoreType.DMA((2,)),
+            pltpu.SemaphoreType.DMA((2,)),
+        ],
         compiler_params=pltpu.CompilerParams(vmem_limit_bytes=60 * 1024 * 1024),
     )(*results)
 

time: 38.5 us -> 37.6 us (0.977)
  Pallas kernels: 37.7 us -> 36.8 us
    pallas_call x1, Pallas kernels: 2.36 us -> 1.42 us  [body(): pl.pallas_call(hand_on, out_shape=out_shape, in_specs=[hbm] * 2, out_spec...]
where the time goes in v4:
time: 37.6 us; the launch traced here: 37.4 us
  Pallas kernels  36.8 us (98%)
  between operations  0.64 us (2%)
    pallas_call x1, Pallas kernels, body(): pl.pallas_call(functools.partial(kernel, slabs, fields), out_shape=out_sh...  35.3 us
    pallas_call x1, Pallas kernels, body(): pl.pallas_call(hand_on, out_shape=out_shape, in_specs=[hbm] * 2, out_spec...  1.42 us

profile of v4, /device:TPU:0, one launch (start us, length us, event | category | flops | bytes accessed | tf_op | source)
XLA Modules:
  0.0 37.4 jit_solution(15624240168959673338)
XLA Ops:
  0.6 35.3 %shard_map.59 = (f32[1,16,64]{2,1,0:T(8,128)}, f32[64,64]{1,0:T(8,128)}) custom-call(bf16[1,2,3,32,2048]{4,3,2,1,0:T(8,128)(2,1)} %snaps_ref.1, s32[1,64]{1,0:T(1,128)} %bitcast.2, s32[64,64]{1,0:T(8,128)} %omega_hbm.1, s32[1,32]{1,0:T(1,128)} %bitcast.3), custom_call_target="tpu_custom_call" | custom-call | tf_op jit(solution)/shard_map/pallas_call | solution.py:324
  36.0 1.4 %shard_map.60 = (f32[1,16,64]{2,1,0:T(8,128)}, f32[64,64]{1,0:T(8,128)}) custom-call(f32[1,16,64]{2,1,0:T(8,128)} %get-tuple-element.4.rows_in, f32[64,64]{1,0:T(8,128)} %get-tuple-element.5.core_in), custom_call_target="tpu_custom_call" | custom-call | tf_op jit(solution)/shard_map/pallas_call | solution.py:354
